TPU v7x, 128 devices: a whole 4x4x4 slice. The times are simulated.
128 devices in a mesh: seq: 32 (over z_hi, y, x), fsdp: 4 (over z_lo, core).
Axes of the slice: x: 4, y: 4, z: 4 (z_hi: 2, z_lo: 2; z = z_hi * 2 + z_lo), core: 2. Of those that a mesh axis runs over, the one named last changes fastest.
Arguments:
- tokens: float32 [4, 8192, 1024], P('fsdp', 'seq'), may hold values from -6 to 6
- token_pos: int32 [4, 8192], P('fsdp', 'seq'), may hold values from 0 to 8183, as said below
- w_in: bfloat16 [1024, 3072], P('seq', 'fsdp'), may hold values from -0.1875 to 0.1875
- w_mix: bfloat16 [1024, 1024], P('seq', 'fsdp'), may hold values from -0.1875 to 0.1875
- w_gate: bfloat16 [1024, 4608], P('seq', 'fsdp'), may hold values from -0.1875 to 0.1875
- w_up: bfloat16 [1024, 4608], P('seq', 'fsdp'), may hold values from -0.1875 to 0.1875
- w_down: bfloat16 [4608, 1024], P('seq', 'fsdp'), may hold values from -0.1875 to 0.1875
- conv_weight: bfloat16 [3, 1024], P(None, 'fsdp'), may hold values from -3 to 3
- norm_gains: bfloat16 [2, 1024], P(None, 'fsdp'), may hold values from 0.5 to 1.5
- cotangent: float32 [4, 8192, 1024], P('fsdp', 'seq'), may hold values from -6 to 6
Outputs:
- block_out: float32 [4, 8192, 1024], P('fsdp', 'seq')
- grad_tokens: float32 [4, 8192, 1024], P('fsdp', 'seq')
- grad_in: float32 [1024, 3072], P('seq', 'fsdp')
- grad_mix: float32 [1024, 1024], P('seq', 'fsdp')
- grad_gate: float32 [1024, 4608], P('seq', 'fsdp')
- grad_up: float32 [1024, 4608], P('seq', 'fsdp')
- grad_down: float32 [4608, 1024], P('seq', 'fsdp')
- grad_conv: float32 [3, 1024], P(None, 'fsdp')
- grad_gains: float32 [2, 1024], P(None, 'fsdp')
Inputs may be any that keep to these rules, and one draw needn't show every extreme that they name: `token_pos`: 0 at the first token of a sequence and one more at each following token of the same sequence within a stream; every stream starts a sequence at its first token.
All inputs are finite; a program needn't handle non-finite values.
Results may differ from a plain program's by a relative error of at most 0.025.
Values may be sent and summed in bfloat16 or wider, within the bound.
No kernel may reach another device: no remote copies, remote signals or barrier semaphores. Data moves between devices by JAX's collectives and lax.ppermute only.
A program may use at most 192 MiB of HBM per device.

v0:
```python
import jax
import jax.numpy as jnp
from jax import lax
from jax.sharding import PartitionSpec as P

EPSILON = 1e-05


def side_by_side(arrays, axis, dim, along):
    ends, at = ([], 0)
    for a in arrays[:-1]:
        at += a.shape[along]
        ends.append(at)
    both = jnp.concatenate(arrays, axis=along)
    return tuple(jnp.split(lax.all_gather(both, axis, axis=dim, tiled=True), ends, axis=along))


def shifted(block, axis, distance):
    devices = range(lax.axis_size(axis))
    route = [(i - distance, i) for i in devices if i - distance in devices]
    return lax.ppermute(block, axis, route)


def in_one_piece(arrays, axis, dim, along):
    ends, at = ([], 0)
    for a in arrays[:-1]:
        at += a.shape[along]
        ends.append(at)
    both = jnp.concatenate(arrays, axis=along)
    return tuple(
        jnp.split(lax.psum_scatter(both, axis, scatter_dimension=dim, tiled=True), ends, axis=along)
    )


def split_up(x, dim, devices):
    shape = x.shape
    tiles = x.reshape(*shape[:dim], devices, shape[dim] // devices, *shape[dim + 1 :])
    return jnp.moveaxis(tiles, dim, 0)


def sum_packed(arrays, axis, dims):
    devices = lax.axis_size(axis)
    tiles = [split_up(a, dim, devices) for a, dim in zip(arrays, dims)]
    lines = jnp.concatenate([b.reshape(devices, -1) for b in tiles], axis=1)
    rows = max(16, -(-lines.shape[1] // 1024) * 8)
    lines = jnp.pad(lines, ((0, 0), (0, rows * 128 - lines.shape[1]))).reshape(-1, 128)
    ravelled, at, outs = (lax.psum_scatter(lines, axis, tiled=True).reshape(-1), 0, [])
    for b in tiles:
        part = b[0]
        outs.append(ravelled[at : at + part.size].reshape(part.shape))
        at += part.size
    return tuple(outs)


def sent_to_all(x, axis):
    copies = jnp.broadcast_to(x, (lax.axis_size(axis), *x.shape))
    return lax.all_to_all(copies, axis, split_axis=0, concat_axis=0, tiled=True)


def of_everyone(x, axis):
    everything = sent_to_all(x, axis)
    return jnp.sum(everything, axis=0)


def packed_total(arrays, axis):
    ravelled, at, outs = (jnp.concatenate([a.reshape(-1) for a in arrays]), 0, [])
    so_far = of_everyone(ravelled, axis)
    for a in arrays:
        outs.append(so_far[at : at + a.size].reshape(a.shape))
        at += a.size
    return tuple(outs)


def norm_forward(values, norm_gain):
    inv_rms = lax.rsqrt(jnp.mean(values * values, axis=-1, keepdims=True) + EPSILON)
    normed = values * inv_rms
    return (normed, inv_rms, (normed * norm_gain).astype(jnp.bfloat16))


def norm_backward(grad_hidden, normed, inv_rms, norm_gain):
    grad_normed = grad_hidden * norm_gain
    inner_mean = jnp.mean(grad_normed * normed, axis=-1, keepdims=True)
    return (inv_rms * (grad_normed - normed * inner_mean), jnp.sum(grad_hidden * normed, axis=0))


def apply_forward(inputs, weight):
    full_weight = lax.all_gather(weight, "seq", axis=0, tiled=True)
    return (jnp.dot(inputs, full_weight, preferred_element_type=jnp.float32), full_weight)


def apply_backward(grad_rows_in, weight):
    return lax.dot_general(
        grad_rows_in, weight, (((1,), (1,)), ((), ())), preferred_element_type=jnp.float32
    )


def weight_grad(inputs, grad_rows_in):
    return lax.dot_general(
        inputs, grad_rows_in, (((0,), (0,)), ((), ())), preferred_element_type=jnp.float32
    )


def local(tokens, token_pos, w_in, w_mix, w_gate, w_up, w_down, conv_weight, norm_gains, cotangent):
    inputs = tokens[0]
    positions = token_pos[0]
    grad_result = cotangent[0]
    columns = (
        lax.all_gather(w_in, "fsdp", axis=1, tiled=True),
        lax.all_gather(w_mix, "fsdp", axis=1, tiled=True),
        *side_by_side((w_gate, w_up), "fsdp", 1, 0),
        *side_by_side((w_down, conv_weight, norm_gains), "fsdp", 1, 0),
    )
    in_cols, mix_cols, gate_cols, up_cols, down_cols, conv_full, gains_full = columns
    ff_dim = gate_cols.shape[1]
    model_dim = inputs.shape[1]
    gate_up = jnp.concatenate([gate_cols, up_cols], axis=1)
    conv_taps = conv_full.astype(jnp.float32)
    gain_rows = gains_full.astype(jnp.float32)
    mask_one = (positions >= 1).astype(jnp.float32)[:, None]
    mask_two = (positions >= 2).astype(jnp.float32)[:, None]
    normed1, inv_one, hidden1 = norm_forward(inputs, gain_rows[0])
    mixed_in, in_kept = apply_forward(hidden1, in_cols)
    b_part = mixed_in[:, :model_dim]
    c_part = mixed_in[:, model_dim : 2 * model_dim]
    x_part = mixed_in[:, 2 * model_dim :]
    product_bx = (b_part * x_part).astype(jnp.bfloat16)
    arrived = shifted(product_bx[-2:], "seq", 1)
    extended = jnp.concatenate([arrived, product_bx], axis=0).astype(jnp.float32)
    current = extended[2:]
    back_one = extended[1:-1]
    back_two = extended[:-2]
    conv_val = (
        conv_taps[2] * current
        + conv_taps[1] * mask_one * back_one
        + conv_taps[0] * mask_two * back_two
    )
    mixer = (c_part * conv_val).astype(jnp.bfloat16)
    branch, mix_kept = apply_forward(mixer, mix_cols)
    middle = inputs + branch
    normed2, inv_two, hidden2 = norm_forward(middle, gain_rows[1])
    gate_up_out, pair_kept = apply_forward(hidden2, gate_up)
    gate_val = gate_up_out[:, :ff_dim]
    up_val = gate_up_out[:, ff_dim:]
    gate_sig = jax.nn.sigmoid(gate_val)
    silu_val = gate_val * gate_sig
    activation = (silu_val * up_val).astype(jnp.bfloat16)
    ffn_out, down_kept = apply_forward(activation, down_cols)
    result = middle + ffn_out
    grad_low = grad_result.astype(jnp.bfloat16)
    grad_down = weight_grad(activation, grad_low)
    grad_act = apply_backward(grad_low, down_kept)
    grad_gate_val = grad_act * up_val * (gate_sig * (1.0 + gate_val * (1.0 - gate_sig)))
    grad_up_val = grad_act * silu_val
    grad_pair = jnp.concatenate([grad_gate_val, grad_up_val], axis=1).astype(jnp.bfloat16)
    grad_gate_up = weight_grad(hidden2, grad_pair)
    grad_hidden2 = apply_backward(grad_pair, pair_kept)
    grad_norm_two, gain_two = norm_backward(grad_hidden2, normed2, inv_two, gain_rows[1])
    grad_middle = grad_result + grad_norm_two
    grad_branch = grad_middle.astype(jnp.bfloat16)
    grad_mixw = weight_grad(mixer, grad_branch)
    grad_mixer = apply_backward(grad_branch, mix_kept)
    grad_c = grad_mixer * conv_val
    grad_cv = grad_mixer * c_part
    lag_one = grad_cv * mask_one
    lag_two = grad_cv * mask_two
    later_one, later_two = shifted((lag_one[:2], lag_two[:2]), "seq", -1)
    ahead_one = jnp.concatenate([lag_one[1:], later_one[:1]], axis=0)
    ahead_two = jnp.concatenate([lag_two[2:], later_two], axis=0)
    grad_bx = conv_taps[2] * grad_cv + conv_taps[1] * ahead_one + conv_taps[0] * ahead_two
    conv_grads = jnp.stack(
        [
            jnp.sum(lag_two * back_two, axis=0),
            jnp.sum(lag_one * back_one, axis=0),
            jnp.sum(grad_cv * current, axis=0),
        ]
    )
    grad_bx_low = lax.optimization_barrier(grad_bx.astype(jnp.bfloat16)).astype(jnp.float32)
    grad_mixed = jnp.concatenate(
        [grad_bx_low * x_part, grad_c, grad_bx_low * b_part], axis=1
    ).astype(jnp.bfloat16)
    grad_inw = weight_grad(hidden1, grad_mixed)
    grad_hidden1 = apply_backward(grad_mixed, in_kept)
    grad_norm_one, gain_one = norm_backward(grad_hidden1, normed1, inv_one, gain_rows[0])
    grad_inputs = grad_middle + grad_norm_one
    gains_grad = jnp.stack([gain_one, gain_two])
    col_sums = (
        lax.psum_scatter(
            grad_inw.astype(jnp.bfloat16), "fsdp", scatter_dimension=1, tiled=True
        ).astype(jnp.float32),
        lax.psum_scatter(
            grad_mixw.astype(jnp.bfloat16), "fsdp", scatter_dimension=1, tiled=True
        ).astype(jnp.float32),
        *tuple(
            (
                part.astype(jnp.float32)
                for part in in_one_piece(
                    (
                        grad_gate_up[:, :ff_dim].astype(jnp.bfloat16),
                        grad_gate_up[:, ff_dim:].astype(jnp.bfloat16),
                    ),
                    "fsdp",
                    1,
                    0,
                )
            )
        ),
        *tuple(
            (
                part.astype(jnp.float32)
                for part in in_one_piece(
                    (
                        grad_down.astype(jnp.bfloat16),
                        conv_grads.astype(jnp.bfloat16),
                        gains_grad.astype(jnp.bfloat16),
                    ),
                    "fsdp",
                    1,
                    0,
                )
            )
        ),
    )
    weight_parts = tuple(
        (
            part.astype(jnp.float32)
            for part in sum_packed(
                (
                    col_sums[0].astype(jnp.bfloat16),
                    col_sums[1].astype(jnp.bfloat16),
                    col_sums[2].astype(jnp.bfloat16),
                    col_sums[3].astype(jnp.bfloat16),
                    col_sums[4].astype(jnp.bfloat16),
                ),
                "seq",
                (0, 0, 0, 0, 0),
            )
        )
    )
    conv_part = col_sums[5]
    gains_part = col_sums[6]
    conv_total, gains_total = packed_total((conv_part, gains_part), "seq")
    return (
        result[None],
        grad_inputs[None],
        weight_parts[0],
        weight_parts[1],
        weight_parts[2],
        weight_parts[3],
        weight_parts[4],
        conv_total,
        gains_total,
    )


def solution(mesh):
    placed = (
        P("fsdp", "seq", None),
        P("fsdp", "seq"),
        P("seq", "fsdp"),
        P("seq", "fsdp"),
        P("seq", "fsdp"),
        P("seq", "fsdp"),
        P("seq", "fsdp"),
        P(None, "fsdp"),
        P(None, "fsdp"),
        P("fsdp", "seq", None),
    )
    return jax.shard_map(
        local,
        mesh=mesh,
        in_specs=placed,
        out_specs=(
            P("fsdp", "seq", None),
            P("fsdp", "seq", None),
            P("seq", "fsdp"),
            P("seq", "fsdp"),
            P("seq", "fsdp"),
            P("seq", "fsdp"),
            P("seq", "fsdp"),
            P(None, "fsdp"),
            P(None, "fsdp"),
        ),
        check_vma=False,
    )
```

profile of v0, /device:TPU:0, one launch (start us, length us, event | category | flops | bytes accessed | tf_op | source)
XLA Modules:
  0.0 1102.3 jit_solution(18137276913831169134)
XLA Ops:
  7.2 7.8 all_gather.25
  15.1 6.0 all_gather.27
  21.2 0.9 pad_maximum_fusion.8
  22.1 7.6 all_gather.29
  29.8 0.9 pad_maximum_fusion.7
  30.7 0.9 pad_maximum_fusion.9
  31.7 6.1 all_gather.24
  37.8 0.7 split.44
  38.8 71.2 %all-gather.5.cloned.1.call-done = bf16[1024,3072]{1,0:T(8,128)(2,1)} async-done(((bf16[32,3072]{1,0:T(8,128)(2,1)}), bf16[1024,3072]{1,0:T(8,128)(2,1)}) %all-gather.5.cloned.1.call-update) | async-done | bytes 6291472 | tf_op jit(solution)/shard_map/all_gather | solution.py:87
  110.0 4.6 fusion.17
  114.9 3.3 collective-permute-start
  118.2 1.1 collective-permute-done
  119.5 1.7 multiply_convert_fusion.5
  121.2 61.7 %all-gather.7.cloned.1.call-done = bf16[1024,1024]{1,0:T(8,128)(2,1)} async-done(((bf16[32,1024]{1,0:T(8,128)(2,1)}), bf16[1024,1024]{1,0:T(8,128)(2,1)}) %all-gather.7.cloned.1.call-update) | async-done | bytes 2097168 | tf_op jit(solution)/shard_map/all_gather | solution.py:87
  182.8 2.6 multiply_reduce_fusion.7
  185.4 167.6 %all-gather.9.cloned.1.call-done = bf16[1024,9216]{1,0:T(8,128)(2,1)} async-done(((bf16[32,9216]{1,0:T(8,128)(2,1)}), bf16[1024,9216]{1,0:T(8,128)(2,1)}) %all-gather.9.cloned.1.call-update) | async-done | bytes 18874384 | tf_op jit(solution)/shard_map/all_gather | solution.py:87
  353.0 14.1 %fusion.18 = f32[256,9216]{1,0:T(8,128)} fusion(bf16[1024,9216]{1,0:T(8,128)(2,1)} %all-gather.9.cloned.1.call-done, f32[256,1024]{1,0:T(8,128)S(1)} %get-tuple-element.44, f32[1024]{0:T(1024)S(1)} %bitcast.71, f32[256]{0:T(256)S(1)} %add_rsqrt_fusion), kind=kOutput, calls=%fused_computation.82 | convolution fusion | flops 4832624640 | bytes 29365248 | tf_op jit(solution)/shard_map/dot_general | solution.py:88
  367.1 97.5 %all-gather.11.cloned.1.call-done = bf16[4608,1024]{1,0:T(8,128)(2,1)} async-done(((bf16[144,1024]{1,0:T(8,128)(2,1)}), bf16[4608,1024]{1,0:T(8,128)(2,1)}) %all-gather.11.cloned.1.call-update) | async-done | bytes 9437200 | tf_op jit(solution)/shard_map/all_gather | solution.py:87
  464.6 13.9 %multiply_convert_fusion.1 = (bf16[256,4608]{1,0:T(8,128)(2,1)}, bf16[256,4608]{1,0:T(8,128)(2,1)}, bf16[256,4608]{1,0:T(8,128)(2,1)}) fusion(f32[256,9216]{1,0:T(8,128)} %fusion.18, bf16[4608,1024]{1,0:T(8,128)(2,1)} %all-gather.11.cloned.1.call-done, f32[1,256,1024]{2,1,0:T(8,128)S(1)} %copy-done.7), kind=kOutput, calls=%fused_computation.7 | convolution fusion | flops 2433613824 | bytes 27000832 | tf_op jit(solution)/shard_map/dot_general | solution.py:92
  478.5 11.4 %multiply_reduce_fusion = (bf16[1024]{0:T(1024)(128)(2,1)S(1)}, f32[256]{0:T(256)S(1)}, f32[256,1024]{1,0:T(8,128)}) fusion(f32[256,1024]{1,0:T(8,128)S(1)} %get-tuple-element.44, f32[256]{0:T(256)S(1)} %add_rsqrt_fusion, f32[1024]{0:T(1024)S(1)} %bitcast.72, bf16[1024,9216]{1,0:T(8,128)(2,1)} %all-gather.9.cloned.1.call-done, ...), kind=kOutput, calls=%fused_computation.31 | convolution fusion | flops 4842847232 | bytes 25698304 | tf_op jit(solution)/shard_map/dot_general | solution.py:92
  489.9 1.5 bitcast_add_fusion
  491.4 2.1 convolution_convert_fusion.3
  493.6 2.5 fusion.11
  497.0 1.3 collective-permute-start.1
  498.3 1.5 collective-permute-start.2
  500.1 2.4 collective-permute-done.1
  502.5 1.9 collective-permute-done.2
  505.2 0.8 copy-done.12
  506.1 4.5 convolution_convert_fusion.2
  510.8 8.4 fusion.27
  519.2 5.9 multiply_reduce_fusion.1
  525.1 39.6 %concatenate.51 = bf16[4613,1024]{1,0:T(8,128)(2,1)} concatenate(bf16[4608,1024]{1,0:T(8,128)(2,1)} %fusion.27, bf16[1,1024]{1,0:T(2,128)(2,1)S(1)} %stack.24, bf16[1,1024]{1,0:T(2,128)(2,1)S(1)} %stack.25, bf16[1,1024]{1,0:T(2,128)(2,1)S(1)} %stack.26, bf16[1,1024]{1,0:T(2,128)(2,1)S(1)} %stack.27, bf16[1,1024]{1,0:T(2,128)(2,1)S(1)} %stack.28), dimensions={0} | concatenate | bytes 18894848 | tf_op jit(solution)/shard_map/concatenate | solution.py:29
  564.8 11.7 %convolution_convert_fusion = bf16[1024,9216]{1,0:T(8,128)(2,1)} fusion(bf16[256,4608]{1,0:T(8,128)(2,1)} %get-tuple-element.24, bf16[256,4608]{1,0:T(8,128)(2,1)} %get-tuple-element.23, f32[256,1024]{1,0:T(8,128)S(1)} %get-tuple-element.44, f32[1024]{0:T(1024)S(1)} %bitcast.74, f32[256]{0:T(256)S(1)} %add_rsqrt_fusion), kind=kOutput, calls=%fused_computation.1 | convolution fusion | flops 4851499008 | bytes 24646656 | tf_op jit(solution)/shard_map/dot_general | solution.py:98
  576.6 7.5 fusion.21
  584.1 7.8 pad_maximum_fusion
  591.8 23.4 %copy.25 = bf16[2048,4608]{0,1:T(8,128)(2,1)} copy(bf16[2048,4608]{1,0:T(8,128)(2,1)} %pad_maximum_fusion) | data formatting | bytes 37748736
  615.5 2.1 reshape_reshape.16
  617.6 2.8 reshape_reshape.15
  620.4 2.7 constant_dynamic-update-slice_fusion.4
  623.1 1.9 constant_dynamic-update-slice_fusion.3
  625.0 52.6 %reduce-scatter.12.cloned.1.call-done = bf16[4613,256]{1,0:T(8,128)(2,1)} async-done(((bf16[4613,1024]{1,0:T(8,128)(2,1)}), bf16[4613,256]{1,0:T(8,128)(2,1)}) %reduce-scatter.12.cloned.1.call-update) | async-done | bytes 2361872 | tf_op jit(solution)/shard_map/reduce_scatter | solution.py:31
  677.6 3.2 split.47
  680.9 4.4 reshape_reshape.19
  685.3 159.4 %reduce-scatter.16.cloned.1.call-done = bf16[1152,2048]{1,0:T(8,128)(2,1)} async-done(((bf16[4608,2048]{1,0:T(8,128)(2,1)}), bf16[1152,2048]{1,0:T(8,128)(2,1)}) %reduce-scatter.16.cloned.1.call-update) | async-done | bytes 4718608
  844.7 5.0 fusion.22
  849.7 4.4 copy.29
  854.0 4.4 reshape_reshape.18
  858.4 4.4 copy.28
  862.7 4.4 reshape_reshape.17
  867.1 3.4 constant_dynamic-update-slice_fusion.2
  870.5 1.6 constant_dynamic-update-slice_fusion.1
  872.1 1.6 constant_dynamic-update-slice_fusion
  873.7 9.5 reshape.121
  883.3 8.0 fusion.2
  892.6 0.8 broadcast_in_dim.8
  893.4 9.4 all-to-all-start
  902.8 2.5 add_bitcast_fusion
  905.3 8.6 all-to-all-done
  915.2 174.6 %reduce-scatter.14.cloned.1.call-done = bf16[1120,128]{1,0:T(8,128)(2,1)} async-done(((bf16[35840,128]{1,0:T(8,128)(2,1)}), bf16[1120,128]{1,0:T(8,128)(2,1)}) %reduce-scatter.14.cloned.1.call-update) | async-done | bytes 286736 | tf_op jit(solution)/shard_map/reduce_scatter | solution.py:47
  1089.9 0.7 slice_convert_fusion.4
  1091.2 0.8 slice_convert_fusion.3
  1092.7 1.0 slice_convert_fusion
  1093.7 0.7 reshape.130
  1094.4 0.7 reshape.129
  (93 shorter events, 8.1 us)
Async XLA Ops:
  7.2 31.4 %copy-start.2 = (f32[1,256,1024]{2,1,0:T(8,128)S(1)}, f32[1,256,1024]{2,1,0:T(8,128)}, u32[]{:S(2)}) copy-start(f32[1,256,1024]{2,1,0:T(8,128)} %param.10) | copy-start | bytes 3145732
  7.2 102.8 %all-gather.5.cloned.1.call-start = ((), (), s32[]{:S(2)}) async-start(), calls=%async_computation.6 | async-start | bytes 6488064 | tf_op jit(solution)/shard_map/all_gather | solution.py:87
  15.1 167.8 %all-gather.7.cloned.1.call-start = ((), (), s32[]{:S(2)}) async-start(), calls=%async_computation.7 | async-start | bytes 2162688 | tf_op jit(solution)/shard_map/all_gather | solution.py:87
  21.1 331.9 %all-gather.9.cloned.1.call-start = ((), (), s32[]{:S(2)}) async-start(), calls=%async_computation.8 | async-start | bytes 19464192 | tf_op jit(solution)/shard_map/all_gather | solution.py:87
  30.7 433.9 %all-gather.11.cloned.1.call-start = ((), (), s32[]{:S(2)}) async-start(), calls=%async_computation.9 | async-start | bytes 9732096 | tf_op jit(solution)/shard_map/all_gather | solution.py:87
  38.5 577.0 %reduce-scatter.10.cloned.1.call-start = ((), (), s32[]{:S(2)}) async-start(), calls=%async_computation.11 | async-start | bytes 2621440 | tf_op jit(solution)/shard_map/reduce_scatter | solution.py:190
  110.0 8.2 copy-start.16
  114.7 4.8 copy-start
  114.9 4.5 collective-permute-start
  353.0 111.6 %copy-start.7 = (f32[1,256,1024]{2,1,0:T(8,128)S(1)}, f32[1,256,1024]{2,1,0:T(8,128)}, u32[]{:S(2)}) copy-start(f32[1,256,1024]{2,1,0:T(8,128)} %param.19) | copy-start | bytes 3145732
  478.5 11.4 %copy-start.8 = (f32[1,256,1024]{2,1,0:T(8,128)S(1)}, f32[1,256,1024]{2,1,0:T(8,128)}, u32[]{:S(2)}) copy-start(f32[1,256,1024]{2,1,0:T(8,128)} %param.19) | copy-start | bytes 3145732
  478.5 12.9 %copy-start.6 = (bf16[256,1024]{1,0:T(8,128)(2,1)S(1)}, bf16[256,1024]{1,0:T(8,128)(2,1)}, u32[]{:S(2)}) copy-start(bf16[256,1024]{1,0:T(8,128)(2,1)} %get-tuple-element.19) | copy-start | bytes 1572868
  493.5 124.1 %reduce-scatter.8.cloned.1.call-start = ((), (), s32[]{:S(2)}) async-start(), calls=%async_computation.10 | async-start | bytes 7864320 | tf_op jit(solution)/shard_map/reduce_scatter | solution.py:187
  493.6 2.5 copy-start.1
  493.6 2.8 copy-start.9
  496.9 8.2 copy-start.10
  497.0 5.5 collective-permute-start.1
  498.3 6.2 collective-permute-start.2
  499.9 6.2 copy-start.3
  505.2 0.8 copy-start.12
  505.2 1.0 copy-start.14
  510.7 167.0 %reduce-scatter.12.cloned.1.call-start = ((), (), s32[]{:S(2)}) async-start(), calls=%async_computation.12 | async-start | bytes 11816960 | tf_op jit(solution)/shard_map/reduce_scatter | solution.py:31
  510.8 8.4 copy-start.11
  510.8 8.4 copy-start.13
  510.8 8.4 copy-start.15
  564.8 279.9 %reduce-scatter.16.cloned.1.call-start = ((), (), s32[]{:S(2)}) async-start(), calls=%async_computation.14 | async-start | bytes 23592960
  615.2 474.7 %reduce-scatter.14.cloned.1.call-start = ((), (), s32[]{:S(2)}) async-start(), calls=%async_computation.13 | async-start | bytes 9461760 | tf_op jit(solution)/shard_map/reduce_scatter | solution.py:47
  867.1 3.4 copy-start.5
  867.1 5.0 copy-start.4
  893.4 20.5 %all-to-all-start = ((f32[32,1,1280]{2,1,0:T(1,128)}), f32[32,1,1280]{2,1,0:T(1,128)S(1)}, u32[]{:S(2)}, u32[]{:S(2)}) async-start(f32[32,1,1280]{2,1,0:T(1,128)} %broadcast_in_dim.8), calls=%async_computation.4 | async-start | bytes 327680 | tf_op jit(solution)/shard_map/all_to_all | solution.py:57
Sparse Core Ops, SparseCore 0:
  15.2 94.8 all-gather.4
  113.1 69.6 all-gather.6
  186.4 166.5 all-gather.8
  355.8 108.7 all-gather.10
  493.6 25.9 reduce-scatter.9
  522.0 63.4 reduce-scatter.7
  588.2 89.4 reduce-scatter.11
  680.2 164.3 reduce-scatter.15
  883.4 206.4 reduce-scatter.13
where the time goes:
time: 1110 us; the launch traced here: 1100 us
  waiting for transfers between devices  799 us (72%)
  local copies, waits for them, and re-layouts  135 us (12%)
  matrix products  89.6 us (8%)
  blocking collectives  27.6 us (2%)
  other arithmetic  20.5 us (2%)
  starting transfers between devices  16.1 us (1%)
  between operations  14.3 us (1%)
    all_gather x4, waiting for transfers between devices, apply_forward(): full_weight = lax.all_gather(weight, 'seq', axis=0, tiled=True)  398 us
    reduce_scatter x1, waiting for transfers between devices, sum_packed(): lax.psum_scatter(lines, axis, tiled=True).reshape(-1)  175 us
    unnamed x10, waiting for transfers between devices  160 us
    reduce_scatter x1, waiting for transfers between devices, in_one_piece(): lax.psum_scatter(both, axis, scatter_dimension=dim, tiled=True)  52.6 us
    unnamed x43, local copies, waits for them, and re-layouts  43.7 us
    concatenate x1, local copies, waits for them, and re-layouts, in_one_piece(): both = jnp.concatenate(arrays, axis=along)  39.6 us
    dot_general x4, matrix products, apply_backward(): lax.dot_general(grad_rows_in, weight, (((1,), (1,)), ((), ())), preferred...  33.6 us
    dot_general x4, matrix products, apply_forward(): jnp.dot(inputs, full_weight, preferred_element_type=jnp.float32)  29.3 us
  transfers between devices with their start and end apart: 13, of which 11 were waited for; matrix products, arithmetic and copies ran while one was open for 15% of the time, Pallas kernels for 0%

commit v1 on v0

--- a/solution.py
+++ b/solution.py
@@ -84,7 +84,9 @@
 
 
 def apply_forward(inputs, weight):
-    full_weight = lax.all_gather(weight, "seq", axis=0, tiled=True)
+    full_weight = jnp.concatenate(
+        lax.all_to_all(jnp.stack([weight] * lax.axis_size("seq")), "seq", 0, 0), axis=0
+    )
     return (jnp.dot(inputs, full_weight, preferred_element_type=jnp.float32), full_weight)
 
 

time: 1110 us -> 1300 us (1.17)
  blocking collectives: 27.6 us -> 170 us
  starting transfers between devices: 16.1 us -> 81.9 us
  waiting for transfers between devices: 799 us -> 775 us
  local copies, waits for them, and re-layouts: 135 us -> 155 us
    all_gather x4 -> x0, waiting for transfers between devices: 398 us -> none  [apply_forward(): full_weight = lax.all_gather(weight, 'seq', axis=0, tiled=True)]
    all_to_all x0 -> x4, waiting for transfers between devices: none -> 251 us  [apply_forward(): lax.all_to_all(jnp.stack([weight] * lax.axis_size('seq')), 'seq', 0, 0)]
    all_gather x2, blocking collectives: 13.8 us -> 141 us  [side_by_side(): lax.all_gather(both, axis, axis=dim, tiled=True)]
    ppermute x3, waiting for transfers between devices: 5.46 us -> 114 us  [shifted(): return lax.ppermute(block, axis, route)]
    all_to_all x0 -> x4, starting transfers between devices: none -> 65.2 us  [apply_forward(): lax.all_to_all(jnp.stack([weight] * lax.axis_size('seq')), 'seq', 0, 0)]
    another operation x0 -> x4, local copies, waits for them, and re-layouts: none -> 16.7 us  [apply_forward(): jnp.stack([weight] * lax.axis_size('seq'))]
    all_gather x1, blocking collectives: 7.8 us -> 23.7 us  [local(): lax.all_gather(w_in, 'fsdp', axis=1, tiled=True)]
    reduce_scatter x1, waiting for transfers between devices: 52.6 us -> 66.2 us  [in_one_piece(): lax.psum_scatter(both, axis, scatter_dimension=dim, tiled=True)]
  transfers between devices with their start and end apart: 13 -> 13, of which waited for: 11 -> 10; matrix products, arithmetic and copies ran while one was open for 15% -> 13% of each run, Pallas kernels for 0% -> 0%
where the time goes in v1:
time: 1300 us
  waiting for transfers between devices  775 us (60%)
  blocking collectives  170 us (13%)
  local copies, waits for them, and re-layouts  155 us (12%)
  matrix products  82.8 us (6%)
  starting transfers between devices  81.9 us (6%)
  other arithmetic  18 us (1%)
  between operations  14.3 us (1%)
    all_to_all x4, waiting for transfers between devices, apply_forward(): lax.all_to_all(jnp.stack([weight] * lax.axis_size('seq')), 'seq', 0, 0)  251 us
    reduce_scatter x1, waiting for transfers between devices, sum_packed(): lax.psum_scatter(lines, axis, tiled=True).reshape(-1)  176 us
    unnamed x6, waiting for transfers between devices  159 us
    all_gather x2, blocking collectives, side_by_side(): lax.all_gather(both, axis, axis=dim, tiled=True)  141 us
    ppermute x3, waiting for transfers between devices, shifted(): return lax.ppermute(block, axis, route)  114 us
    reduce_scatter x1, waiting for transfers between devices, in_one_piece(): lax.psum_scatter(both, axis, scatter_dimension=dim, tiled=True)  66.2 us
    all_to_all x4, starting transfers between devices, apply_forward(): lax.all_to_all(jnp.stack([weight] * lax.axis_size('seq')), 'seq', 0, 0)  65.2 us
    unnamed x63, local copies, waits for them, and re-layouts  48.1 us
  transfers between devices with their start and end apart: 13, of which 10 were waited for; matrix products, arithmetic and copies ran while one was open for 13% of the time, Pallas kernels for 0%

profile of v1, /device:TPU:0, one launch (start us, length us, event | category | flops | bytes accessed | tf_op | source)
XLA Modules:
  0.0 1297.2 jit_solution(1370492396322809893)
XLA Ops:
  7.2 5.5 all_gather.14
  12.7 1.6 stack.26
  14.3 10.7 all-to-all-start.1
  25.0 23.7 %all_gather.13 = bf16[32,3072]{1,0:T(8,128)(2,1)S(1)} all-gather(bf16[32,768]{1,0:T(8,128)(2,1)S(1)} %copy-done.23), channel_id=1, replica_groups=mesh['seq'=32,'fsdp'=4] {'fsdp'}, dimensions={1}, use_global_device_ids=true | all-gather | bytes 245760 | tf_op jit(solution)/shard_map/all_gather | solution.py:110
  48.7 6.1 all-to-all-done.1
  54.8 3.4 stack.25
  58.2 6.9 all-to-all-start
  65.2 38.0 %all_gather.15 = bf16[64,4608]{1,0:T(8,128)(2,1)S(1)} all-gather(bf16[64,1152]{1,0:T(8,128)(2,1)S(1)} %pad_maximum_fusion.8), channel_id=1, replica_groups=mesh['seq'=32,'fsdp'=4] {'fsdp'}, dimensions={1}, use_global_device_ids=true | all-gather | bytes 737280 | tf_op jit(solution)/shard_map/all_gather | solution.py:15
  103.3 52.9 %all-to-all-done = bf16[32,32,3072]{2,1,0:T(8,128)(2,1)} async-done(((bf16[32,32,3072]{2,1,0:T(8,128)(2,1)}), bf16[32,32,3072]{2,1,0:T(8,128)(2,1)}, u32[]{:S(2)}, u32[]{:S(2)}) %all-to-all-start) | async-done | bytes 6291488 | tf_op jit(solution)/shard_map/all_to_all | solution.py:88
  156.2 6.8 stack.27
  163.0 8.5 all-to-all-start.2
  171.5 103.0 %all_gather.12 = bf16[149,1024]{1,0:T(8,128)(2,1)S(1)} all-gather(bf16[149,256]{1,0:T(8,128)(2,1)S(1)} %pad_maximum_fusion.9), channel_id=1, replica_groups=mesh['seq'=32,'fsdp'=4] {'fsdp'}, dimensions={1}, use_global_device_ids=true | all-gather | bytes 381440 | tf_op jit(solution)/shard_map/all_gather | solution.py:15
  274.6 191.9 %all-to-all-done.2 = bf16[32,32,9216]{2,1,0:T(8,128)(2,1)} async-done(((bf16[32,32,9216]{2,1,0:T(8,128)(2,1)}), bf16[32,32,9216]{2,1,0:T(8,128)(2,1)}, u32[]{:S(2)}, u32[]{:S(2)}) %all-to-all-start.2) | async-done | bytes 18874400 | tf_op jit(solution)/shard_map/all_to_all | solution.py:88
  466.6 4.9 stack.28
  471.4 39.1 %all-to-all-start.3 = ((bf16[32,144,1024]{2,1,0:T(8,128)(2,1)}), bf16[32,144,1024]{2,1,0:T(8,128)(2,1)}, u32[]{:S(2)}, u32[]{:S(2)}) async-start(bf16[32,144,1024]{2,1,0:T(8,128)(2,1)} %stack.28), calls=%async_computation.3 | async-start | bytes 18874368 | tf_op jit(solution)/shard_map/all_to_all | solution.py:88
  510.8 4.6 fusion.11
  515.7 4.1 collective-permute-start
  519.8 108.9 %collective-permute-done = bf16[2,1024]{1,0:T(2,128)(2,1)S(1)} collective-permute-done((bf16[2,1024]{1,0:T(2,128)(2,1)S(1)}, bf16[2,1024]{1,0:T(2,128)(2,1)S(1)}, u32[]{:S(2)}, u32[]{:S(2)}) %collective-permute-start) | collective-permute-done | bytes 4128 | tf_op jit(solution)/shard_map/ppermute | solution.py:21
  628.8 1.5 multiply_convert_fusion.6
  631.1 0.9 copy-done
  632.1 14.0 %fusion.26 = f32[256,9216]{1,0:T(8,128)} fusion(bf16[1024,9216]{1,0:T(8,128)(2,1)} %bitcast.11, f32[256,1024]{1,0:T(8,128)S(1)} %get-tuple-element.44, f32[1024]{0:T(1024)S(1)} %bitcast.74, f32[256]{0:T(256)S(1)} %add_rsqrt_fusion), kind=kOutput, calls=%fused_computation.90 | convolution fusion | flops 4832624640 | bytes 29365248 | tf_op jit(solution)/shard_map/dot_general | solution.py:90
  646.1 10.7 multiply_convert_fusion.1
  656.7 11.3 multiply_reduce_fusion
  668.0 1.8 bitcast_add_fusion
  669.9 1.0 copy-done.3
  670.9 2.1 convolution_convert_fusion.3
  673.1 2.1 fusion.20
  676.2 1.3 collective-permute-start.1
  677.5 1.5 collective-permute-start.2
  679.3 2.8 collective-permute-done.1
  682.1 1.9 collective-permute-done.2
  685.7 4.5 convolution_convert_fusion.2
  690.4 1.1 copy-done.14
  691.5 7.0 fusion.33
  698.4 5.9 multiply_reduce_fusion.1
  704.4 39.7 %concatenate.51 = bf16[4613,1024]{1,0:T(8,128)(2,1)} concatenate(bf16[4608,1024]{1,0:T(8,128)(2,1)} %fusion.33, bf16[1,1024]{1,0:T(2,128)(2,1)S(1)} %stack.29, bf16[1,1024]{1,0:T(2,128)(2,1)S(1)} %stack.30, bf16[1,1024]{1,0:T(2,128)(2,1)S(1)} %stack.31, bf16[1,1024]{1,0:T(2,128)(2,1)S(1)} %stack.32, bf16[1,1024]{1,0:T(2,128)(2,1)S(1)} %stack.33), dimensions={0} | concatenate | bytes 18894848 | tf_op jit(solution)/shard_map/concatenate | solution.py:29
  744.1 1.1 copy-done.2
  745.3 11.8 convolution_convert_fusion
  757.0 7.5 fusion.28
  764.5 7.8 pad_maximum_fusion
  772.3 24.6 %copy.25 = bf16[2048,4608]{0,1:T(8,128)(2,1)} copy(bf16[2048,4608]{1,0:T(8,128)(2,1)} %pad_maximum_fusion) | data formatting | bytes 37748736
  797.3 1.3 reshape_reshape.16
  798.6 2.8 reshape_reshape.15
  801.4 2.7 constant_dynamic-update-slice_fusion.4
  804.0 0.8 constant_dynamic-update-slice_fusion.3
  804.9 66.2 %reduce-scatter.12.cloned.1.call-done = bf16[4613,256]{1,0:T(8,128)(2,1)} async-done(((bf16[4613,1024]{1,0:T(8,128)(2,1)}), bf16[4613,256]{1,0:T(8,128)(2,1)}) %reduce-scatter.12.cloned.1.call-update) | async-done | bytes 2361872 | tf_op jit(solution)/shard_map/reduce_scatter | solution.py:31
  871.1 3.2 split.47
  874.3 4.4 reshape_reshape.19
  878.7 159.3 %reduce-scatter.16.cloned.1.call-done = bf16[1152,2048]{1,0:T(8,128)(2,1)} async-done(((bf16[4608,2048]{1,0:T(8,128)(2,1)}), bf16[1152,2048]{1,0:T(8,128)(2,1)}) %reduce-scatter.16.cloned.1.call-update) | async-done | bytes 4718608
  1038.0 5.0 fusion.29
  1043.0 4.4 copy.29
  1047.4 4.4 reshape_reshape.18
  1051.7 4.4 copy.28
  1056.1 4.4 reshape_reshape.17
  1060.5 3.4 constant_dynamic-update-slice_fusion.2
  1063.9 1.6 constant_dynamic-update-slice_fusion.1
  1065.5 1.6 constant_dynamic-update-slice_fusion
  1067.1 9.5 reshape.160
  1076.7 8.0 fusion.2
  1086.9 9.4 all-to-all-start.4
  1096.3 2.5 add_bitcast_fusion
  1098.8 8.6 all-to-all-done.4
  1108.7 176.1 %reduce-scatter.14.cloned.1.call-done = bf16[1120,128]{1,0:T(8,128)(2,1)} async-done(((bf16[35840,128]{1,0:T(8,128)(2,1)}), bf16[1120,128]{1,0:T(8,128)(2,1)}) %reduce-scatter.14.cloned.1.call-update) | async-done | bytes 286736 | tf_op jit(solution)/shard_map/reduce_scatter | solution.py:47
  1287.6 1.0 slice_convert_fusion
  (113 shorter events, 13.3 us)
Async XLA Ops:
  7.2 17.8 %copy-start.23 = (bf16[32,768]{1,0:T(8,128)(2,1)S(1)}, bf16[32,768]{1,0:T(8,128)(2,1)}, u32[]{:S(2)}) copy-start(bf16[32,768]{1,0:T(8,128)(2,1)} %param.12) | copy-start | bytes 147460
  14.3 40.5 %all-to-all-start.1 = ((bf16[32,32,1024]{2,1,0:T(8,128)(2,1)}), bf16[32,32,1024]{2,1,0:T(8,128)(2,1)S(1)}, u32[]{:S(2)}, u32[]{:S(2)}) async-start(bf16[32,32,1024]{2,1,0:T(8,128)(2,1)} %stack.26), calls=%async_computation.1 | async-start | bytes 4194304 | tf_op jit(solution)/shard_map/all_to_all | solution.py:88
  58.2 6.9 copy-start.21
  58.2 6.9 copy-start.22
  58.2 98.0 %all-to-all-start = ((bf16[32,32,3072]{2,1,0:T(8,128)(2,1)}), bf16[32,32,3072]{2,1,0:T(8,128)(2,1)}, u32[]{:S(2)}, u32[]{:S(2)}) async-start(bf16[32,32,3072]{2,1,0:T(8,128)(2,1)} %stack.25), calls=%async_computation | async-start | bytes 12582912 | tf_op jit(solution)/shard_map/all_to_all | solution.py:88
  163.0 8.5 copy-start.20
  163.0 8.5 copy-start.24
  163.0 8.5 copy-start.25
  163.0 303.6 %all-to-all-start.2 = ((bf16[32,32,9216]{2,1,0:T(8,128)(2,1)}), bf16[32,32,9216]{2,1,0:T(8,128)(2,1)}, u32[]{:S(2)}, u32[]{:S(2)}) async-start(bf16[32,32,9216]{2,1,0:T(8,128)(2,1)} %stack.27), calls=%async_computation.2 | async-start | bytes 37748736 | tf_op jit(solution)/shard_map/all_to_all | solution.py:88
  471.4 39.2 %copy-start.7 = (f32[1,256,1024]{2,1,0:T(8,128)S(1)}, f32[1,256,1024]{2,1,0:T(8,128)}, u32[]{:S(2)}) copy-start(f32[1,256,1024]{2,1,0:T(8,128)} %param.10) | copy-start | bytes 3145732
  471.4 174.6 %all-to-all-start.3 = ((bf16[32,144,1024]{2,1,0:T(8,128)(2,1)}), bf16[32,144,1024]{2,1,0:T(8,128)(2,1)}, u32[]{:S(2)}, u32[]{:S(2)}) async-start(bf16[32,144,1024]{2,1,0:T(8,128)(2,1)} %stack.28), calls=%async_computation.3 | async-start | bytes 18874368 | tf_op jit(solution)/shard_map/all_to_all | solution.py:88
  510.5 286.7 %reduce-scatter.10.cloned.1.call-start = ((), (), s32[]{:S(2)}) async-start(), calls=%async_computation.11 | async-start | bytes 2621440 | tf_op jit(solution)/shard_map/reduce_scatter | solution.py:192
  510.8 8.9 copy-start.26
  515.5 114.8 %copy-start.5 = (f32[256,3072]{1,0:T(8,128)}, f32[256,3072]{1,0:T(8,128)S(1)}, u32[]{:S(2)}) copy-start(f32[256,3072]{1,0:T(8,128)S(1)} %fusion.11) | copy-start | bytes 9437188
  515.5 114.8 %copy-start.8 = (f32[1,256,1024]{2,1,0:T(8,128)S(1)}, f32[1,256,1024]{2,1,0:T(8,128)}, u32[]{:S(2)}) copy-start(f32[1,256,1024]{2,1,0:T(8,128)} %param.10) | copy-start | bytes 3145732
  515.7 113.0 %collective-permute-start = (bf16[2,1024]{1,0:T(2,128)(2,1)S(1)}, bf16[2,1024]{1,0:T(2,128)(2,1)S(1)}, u32[]{:S(2)}, u32[]{:S(2)}) collective-permute-start(bf16[2,1024]{1,0:T(2,128)(2,1)S(1)} %slice.151), channel_id=1, source_target_pairs={{0,4},{4,8},{8,12},{12,16},{16,20},{20,24},{24,28},{28,32},{32,36}... | collective-permute-start | bytes 12296 | tf_op jit(solution)/shard_map/ppermute | solution.py:21
  630.3 0.8 copy-start.12
  631.1 1.0 copy-start
  646.1 10.7 copy-start.1
  656.7 14.2 %copy-start.13 = (bf16[256,1024]{1,0:T(8,128)(2,1)S(1)}, bf16[256,1024]{1,0:T(8,128)(2,1)}, u32[]{:S(2)}) copy-start(bf16[256,1024]{1,0:T(8,128)(2,1)} %copy-done.12) | copy-start | bytes 1572868
  669.9 1.0 copy-start.3
  673.1 125.5 %reduce-scatter.8.cloned.1.call-start = ((), (), s32[]{:S(2)}) async-start(), calls=%async_computation.10 | async-start | bytes 7864320 | tf_op jit(solution)/shard_map/reduce_scatter | solution.py:189
  673.1 2.2 copy-start.6
  673.1 2.5 copy-start.15
  676.2 5.9 collective-permute-start.1
  677.5 6.6 collective-permute-start.2
  679.1 6.6 copy-start.9
  684.8 0.8 copy-start.16
  684.8 1.0 copy-start.18
  690.2 1.2 copy-start.14
  690.3 180.8 %reduce-scatter.12.cloned.1.call-start = ((), (), s32[]{:S(2)}) async-start(), calls=%async_computation.12 | async-start | bytes 11816960 | tf_op jit(solution)/shard_map/reduce_scatter | solution.py:31
  691.5 7.0 copy-start.17
  691.5 7.0 copy-start.19
  744.0 1.2 copy-start.2
  744.1 293.9 %reduce-scatter.16.cloned.1.call-start = ((), (), s32[]{:S(2)}) async-start(), calls=%async_computation.14 | async-start | bytes 23592960
  797.0 487.8 %reduce-scatter.14.cloned.1.call-start = ((), (), s32[]{:S(2)}) async-start(), calls=%async_computation.13 | async-start | bytes 9461760 | tf_op jit(solution)/shard_map/reduce_scatter | solution.py:47
  1060.5 3.4 copy-start.11
  1060.5 5.0 copy-start.10
  1076.7 19.6 %copy-start.4 = (f32[256,1024]{1,0:T(8,128)S(1)}, f32[256,1024]{1,0:T(8,128)}, u32[]{:S(2)}) copy-start(f32[256,1024]{1,0:T(8,128)} %copy-done.3) | copy-start | bytes 3145732
  1086.9 20.5 %all-to-all-start.4 = ((f32[32,1,1280]{2,1,0:T(1,128)}), f32[32,1,1280]{2,1,0:T(1,128)S(1)}, u32[]{:S(2)}, u32[]{:S(2)}) async-start(f32[32,1,1280]{2,1,0:T(1,128)} %broadcast_in_dim.8), calls=%async_computation.8 | async-start | bytes 327680 | tf_op jit(solution)/shard_map/all_to_all | solution.py:57
Sparse Core Ops, SparseCore 0:
  673.2 39.6 reduce-scatter.9
  715.5 63.4 reduce-scatter.7
  781.6 89.4 reduce-scatter.11
  873.6 164.3 reduce-scatter.15
  1076.8 207.9 reduce-scatter.13
